TPU v7x, 128 devices: a whole 4x4x4 slice. The times are simulated.
128 devices in a mesh: tile: 32 (over x, y, core), mem: 4 (over z).
Axes of the slice: x: 4, y: 4, z: 4, core: 2. Of those that a mesh axis runs over, the one named last changes fastest.
Arguments:
- control: bfloat16 [80, 1, 1440, 720], P('mem', None, 'tile'), may hold values from -6 to 6
- perturb: bfloat16 [80, 1, 1440, 720], P('mem', None, 'tile'), may hold values from -6 to 6
- lon_taps: bfloat16 [17], replicated, may hold values from 0.026367188 to 0.07910156
- lat_taps: bfloat16 [17], replicated, may hold values from 0.026367188 to 0.07910156
- innov: float32 [32, 32, 256], P('tile'), may hold values from -6 to 6
- inv_var: float32 [32, 32, 256], P('tile'), may hold values from 1 to 8
- cell_index: int32 [32, 32, 256], P('tile'), may hold values from 0 to 32399, as said below
- counts: int32 [32, 32], P('tile'), may hold values from 0 to 256, as said below
Outputs:
- gradient: float32 [80, 1, 1440, 720], P('mem', None, 'tile')
Inputs may be any that keep to these rules, and one draw needn't show every extreme that they name: `cell_index`: an observation's cell within its owning tile, level * 45 * 720 + longitude within the tile * 720 + latitude; both ends are taken. `counts`: live slots per pair of tiles; some pair fills all 256 slots in every draw, and some owning tiles receive far more than others.
All inputs are finite; a program needn't handle non-finite values.
Results may differ from a plain program's by a relative error of at most 0.00066.
Values may be sent and summed in bfloat16 or wider, within the bound.
A program may use at most 64 MiB of HBM per device.

v0:
```python
import math

import jax
import jax.numpy as jnp
from jax import lax
from jax.sharding import PartitionSpec as P


def extended_2(block, sides, width):
    for axis, dim in sides:
        count = lax.axis_size(axis)
        forward = [(i, i + 1) for i in range(count - 1)]
        forward.append((count - 1, 0))
        backward = [(target, source) for source, target in forward]
        low = lax.ppermute(
            lax.slice_in_dim(block, block.shape[dim] - width, None, axis=dim), axis, forward
        )
        high = lax.ppermute(lax.slice_in_dim(block, 0, width, axis=dim), axis, backward)
        block = jnp.concatenate([low, block, high], axis=dim)
    return block


def band_from(offsets, tap_weights):
    radius = tap_weights.shape[0] - 1
    taps = tap_weights.astype(jnp.float32)
    band = jnp.zeros(offsets.shape, jnp.float32)
    for offset in range(radius + 1):
        band = band + jnp.where(offsets == offset, taps[offset], 0.0)
    return band.astype(jnp.bfloat16)


def lon_band(tap_weights, lon_cells):
    radius = tap_weights.shape[0] - 1
    row_ids = lax.broadcasted_iota(jnp.int32, (lon_cells, lon_cells + 2 * radius), 0)
    col_ids = lax.broadcasted_iota(jnp.int32, (lon_cells, lon_cells + 2 * radius), 1)
    return band_from(jnp.abs(col_ids - row_ids - radius), tap_weights)


def lat_block_band(tap_weights, block_cells):
    radius = tap_weights.shape[0] - 1
    row_ids = lax.broadcasted_iota(jnp.int32, (block_cells + 2 * radius, block_cells), 0)
    col_ids = lax.broadcasted_iota(jnp.int32, (block_cells + 2 * radius, block_cells), 1)
    return band_from(jnp.abs(row_ids - radius - col_ids), tap_weights)


def localize(extended, band_lon, band_blocks, radius, block_cells):
    along = jnp.einsum(
        "ij,mljk->mlik", band_lon, extended, preferred_element_type=jnp.float32
    ).astype(jnp.bfloat16)
    members_here, levels, lon_cells, lat_cells = along.shape
    padded = jnp.pad(along, ((0, 0), (0, 0), (0, 0), (radius, radius)))
    block_count = lat_cells // block_cells
    windows = jnp.stack(
        [
            padded[:, :, :, block * block_cells : block * block_cells + block_cells + 2 * radius]
            for block in range(block_count)
        ],
        axis=3,
    )
    result = jnp.einsum("mlibk,kq->mlibq", windows, band_blocks, preferred_element_type=jnp.float32)
    return result.reshape(members_here, levels, lon_cells, lat_cells)


def pick_cells(field_rows, row_index, col_index, block_rows):
    row_count, col_count = field_rows.shape
    field_cols = field_rows.T

    def pick_one_block(indices):
        rows_here, cols_here = indices
        onehot_rows = (
            rows_here[:, None] == jnp.arange(row_count, dtype=jnp.int32)[None, :]
        ).astype(jnp.float32)
        onehot_cols = (
            cols_here[:, None] == jnp.arange(col_count, dtype=jnp.int32)[None, :]
        ).astype(jnp.float32)
        picked = jnp.dot(
            onehot_cols,
            field_cols,
            precision=lax.Precision.HIGHEST,
            preferred_element_type=jnp.float32,
        )
        return jnp.sum(picked * onehot_rows, axis=1)

    values = lax.map(
        pick_one_block, (row_index.reshape(-1, block_rows), col_index.reshape(-1, block_rows))
    )
    return values.reshape(-1)


def spread_cells(misfit, row_index, col_index, row_count, col_count, block_rows):

    def spread_one_block(total, items):
        rows_here, cols_here, values = items
        onehot_rows = (
            rows_here[:, None] == jnp.arange(row_count, dtype=jnp.int32)[None, :]
        ).astype(jnp.float32)
        onehot_cols = (
            cols_here[:, None] == jnp.arange(col_count, dtype=jnp.int32)[None, :]
        ).astype(jnp.float32)
        weighted = onehot_rows * values[:, None]
        return (
            total
            + jnp.dot(
                weighted.T,
                onehot_cols,
                precision=lax.Precision.HIGHEST,
                preferred_element_type=jnp.float32,
            ),
            None,
        )

    start = jnp.zeros((row_count, col_count), jnp.float32)
    items = (
        row_index.reshape(-1, block_rows),
        col_index.reshape(-1, block_rows),
        misfit.reshape(-1, block_rows),
    )
    total, _ = lax.scan(spread_one_block, start, items)
    return total


def local(control, perturb, lon_taps, lat_taps, innov, inv_var, cell_index, counts):
    members_here, levels, lon_cells, lat_cells = control.shape
    radius = lon_taps.shape[0] - 1
    block_cells = 144
    band_lon = lon_band(lon_taps, lon_cells)
    band_blocks = lat_block_band(lat_taps, block_cells)
    extended = extended_2(control, (("tile", 2),), radius)
    smoothed = localize(extended, band_lon, band_blocks, radius, block_cells)
    member_sum = jnp.sum(perturb.astype(jnp.float32) * smoothed, axis=0)
    slot_ids = lax.broadcasted_iota(jnp.int32, innov.shape, 2)
    is_live = slot_ids < counts[:, :, None]
    weights = jnp.where(is_live, inv_var, 0.0)
    received = (
        lax.all_to_all(innov, "tile", split_axis=1, concat_axis=0, tiled=True),
        lax.all_to_all(weights, "tile", split_axis=1, concat_axis=0, tiled=True),
        lax.all_to_all(cell_index, "tile", split_axis=1, concat_axis=0, tiled=True),
    )
    observed = received[0].reshape(-1)
    weight_recv = received[1].reshape(-1)
    cells_hit = received[2].reshape(-1)
    row_index = cells_hit // lat_cells
    col_index = cells_hit % lat_cells
    row_count = levels * lon_cells
    block_rows = math.gcd(observed.shape[0], 1024)
    increment = lax.psum(member_sum, "mem")
    at_cells = pick_cells(increment.reshape(row_count, lat_cells), row_index, col_index, block_rows)
    misfit = weight_recv * (at_cells - observed)
    spread = spread_cells(misfit, row_index, col_index, row_count, lat_cells, block_rows)
    spread = spread.reshape(levels, lon_cells, lat_cells)
    products = (perturb.astype(jnp.float32) * spread[None]).astype(jnp.bfloat16)
    wide_products = extended_2(products, (("tile", 2),), radius)
    return control.astype(jnp.float32) + localize(
        wide_products, band_lon, band_blocks, radius, block_cells
    )


def solution(mesh):
    return jax.shard_map(
        local,
        mesh=mesh,
        in_specs=(
            P("mem", None, "tile", None),
            P("mem", None, "tile", None),
            P(),
            P(),
            P("tile", None, None),
            P("tile", None, None),
            P("tile", None, None),
            P("tile", None),
        ),
        out_specs=P("mem", None, "tile", None),
        check_vma=False,
    )
```

profile of v0, /device:TPU:0, one launch (start us, length us, event | category | flops | bytes accessed | tf_op | source)
XLA Modules:
  0.0 220.2 jit_solution(9233047360821560978)
XLA Ops:
  8.1 5.1 %collective-permute-start.1 = (bf16[20,1,16,720]{3,2,0,1:T(8,128)(2,1)S(1)}, bf16[20,1,16,720]{3,2,0,1:T(8,128)(2,1)}, u32[]{:S(2)}, u32[]{:S(2)}) collective-permute-start(bf16[20,1,16,720]{3,2,0,1:T(8,128)(2,1)S(1)} %get-tuple-element.118), channel_id=1, source_target_pairs={{4,0},{8,4},{12,8},{16,12},{20,16},{24,20},{28,24},{32,28},{36,32}... | collective-permute-start | bytes 1382408 | tf_op jit(solution)/shard_map/ppermute | solution.py:18
  14.6 4.1 %all-to-all-start = ((s32[1,32,256]{2,0,1:T(1,128)}), s32[1,32,256]{2,0,1:T(1,128)S(1)}, u32[]{:S(2)}, u32[]{:S(2)}) async-start(s32[1,32,256]{2,0,1:T(1,128)} %copy.42), calls=%async_computation | async-start | bytes 65536 | tf_op jit(solution)/shard_map/all_to_all | solution.py:137
  18.7 2.0 fusion.169
  22.1 2.0 fusion.168
  26.1 6.8 %all-to-all-start.1 = ((f32[1,32,256]{2,0,1:T(1,128)}), f32[1,32,256]{2,0,1:T(1,128)S(1)}, u32[]{:S(2)}, u32[]{:S(2)}) async-start(f32[1,32,256]{2,0,1:T(1,128)} %compare_select_fusion), calls=%async_computation.1 | async-start | bytes 65536 | tf_op jit(solution)/shard_map/all_to_all | solution.py:136
  33.2 7.2 %all-to-all-done.1 = f32[1,32,256]{2,0,1:T(1,128)S(1)} async-done(((f32[1,32,256]{2,0,1:T(1,128)}), f32[1,32,256]{2,0,1:T(1,128)S(1)}, u32[]{:S(2)}, u32[]{:S(2)}) %all-to-all-start.1) | async-done | bytes 32800 | tf_op jit(solution)/shard_map/all_to_all | solution.py:136
  40.4 3.8 %all-to-all-start.2 = ((f32[1,32,256]{2,0,1:T(1,128)}), f32[1,32,256]{2,0,1:T(1,128)S(1)}, u32[]{:S(2)}, u32[]{:S(2)}) async-start(f32[1,32,256]{2,0,1:T(1,128)} %copy.50), calls=%async_computation.2 | async-start | bytes 65536 | tf_op jit(solution)/shard_map/all_to_all | solution.py:135
  44.8 6.9 %all-to-all-done.2 = f32[1,32,256]{2,0,1:T(1,128)S(1)} async-done(((f32[1,32,256]{2,0,1:T(1,128)}), f32[1,32,256]{2,0,1:T(1,128)S(1)}, u32[]{:S(2)}, u32[]{:S(2)}) %all-to-all-start.2) | async-done | bytes 32800 | tf_op jit(solution)/shard_map/all_to_all | solution.py:135
  51.8 12.4 %fusion.30 = bf16[20,1,45,720]{3,2,0,1:T(8,128)(2,1)S(1)} fusion(bf16[20,1,16,720]{3,2,0,1:T(8,128)(2,1)} %collective-permute-done.1, bf16[20,1,45,720]{3,2,0,1:T(8,128)(2,1)S(1)} %bitcast.146, bf16[20,1,16,720]{3,2,0,1:T(8,128)(2,1)} %collective-permute-done, f32[]{:T(128)} %bitcast.26, f32[]{:T(128)} %bitcast.25, f32[]{:T(128)} %bitcast.24, f32[]{:T(128)} %bitcast.23, ...), kind=kOutput, calls=%fused_computation.44 | convolution fusion | flops 107279912 | bytes 3513668 | tf_op jit(solution)/shard_map/ij,mljk->mlik/dot_general | solution.py:47
  65.1 11.7 %fusion.26 = f32[20,45,5,144]{3,1,2,0:T(8,128)S(1)} fusion(f32[]{:T(128)} %bitcast.53, f32[]{:T(128)} %bitcast.52, f32[]{:T(128)} %bitcast.51, f32[]{:T(128)} %bitcast.50, f32[]{:T(128)} %bitcast.49, f32[]{:T(128)} %bitcast.48, f32[]{:T(128)} %bitcast.47, f32[]{:T(128)} %bitcast.46, f32[]{:T(128)} %bitcast.45, f32[]{:T(128)} %bitcast.44, f32[]{:T(128)} %bitcast.43, ...), kind=kOutput, calls=%fused_computation.40 | convolution fusion | flops 229439232 | bytes 4176772 | tf_op jit(solution)/shard_map/mlibk,kq->mlibq/dot_general | solution.py:60
  76.9 6.4 %copy.48 = f32[20,45,5,144]{3,2,1,0:T(8,128)} copy(f32[20,45,5,144]{3,1,2,0:T(8,128)S(1)} %fusion.26) | data formatting | bytes 5184000 | tf_op jit(solution)/shard_map/mlibk,kq->mlibq/dot_general | solution.py:60
  83.3 4.9 %reshape.117 = f32[20,1,45,720]{3,2,0,1:T(8,128)S(1)} reshape(f32[20,45,5,144]{3,2,1,0:T(8,128)} %copy.48) | data formatting | bytes 5184000 | tf_op jit(solution)/shard_map/reshape | solution.py:61
  88.1 2.4 %fusion.12 = f32[45,720]{1,0:T(8,128)} fusion(f32[20,1,45,720]{3,2,0,1:T(8,128)S(1)} %reshape.117, bf16[20,1,45,720]{3,2,1,0:T(8,128)(2,1)} %param.13), kind=kLoop, calls=%fused_computation.23 | loop fusion | flops 1911600 | bytes 4017600 | tf_op jit(solution)/shard_map/reduce_sum | solution.py:130
  90.6 40.2 %all-reduce.4.cloned.1.call-done = f32[720,45]{0,1:T(8,128)} async-done(((f32[720,45]{0,1:T(8,128)}), f32[720,45]{0,1:T(8,128)}) %all-reduce.4.cloned.1.call-update) | async-done | bytes 129616 | tf_op jit(solution)/shard_map/psum | solution.py:146
  131.9 15.6 %while.21 = (s32[]{:T(128)}, f32[8,1024]{1,0:T(8,128)S(1)}, s32[8,1024]{1,0:T(8,128)S(1)}, s32[8,1024]{1,0:T(8,128)S(1)}, f32[720,45]{1,0:T(8,128)S(1)}, /*index=5*/s32[]{:T(128)}, s32[]{:T(128)}) while((s32[]{:T(128)}, f32[8,1024]{1,0:T(8,128)S(1)}, s32[8,1024]{1,0:T(8,128)S(1)}, s32[8,1024]{1,0:T(8,128)S(1)}, f32[720,45]{1,0:T(8,128)S(1)}, ...), condition=%wide.region_4.5_spmd, body=%wide.region_2.4_spmd.sunk | while | flops 399005696 | bytes 166549 | solution.py:84
  131.9 1.8 fusion.178
  133.9 1.8 fusion.178
  135.8 1.8 fusion.178
  137.8 1.8 fusion.178
  139.7 1.8 fusion.178
  141.7 1.8 fusion.178
  143.6 1.8 fusion.178
  145.6 1.8 fusion.178
  147.5 12.5 %while.22 = (s32[]{:T(128)}, f32[45,720]{1,0:T(8,128)S(1)}, s32[8,1024]{1,0:T(8,128)S(1)}, f32[8,1024]{1,0:T(8,128)S(1)}, s32[8,1024]{1,0:T(8,128)S(1)}, /*index=5*/s32[]{:T(128)}, s32[]{:T(128)}) while((s32[]{:T(128)}, f32[45,720]{1,0:T(8,128)S(1)}, s32[8,1024]{1,0:T(8,128)S(1)}, f32[8,1024]{1,0:T(8,128)S(1)}, ...), condition=%wide.region_6.7_spmd.clone, body=%wide.region_5.6_spmd.clone.sunk | while | flops 399025440 | bytes 296159 | solution.py:118
  160.5 5.1 %collective-permute-start.3 = (bf16[20,1,16,720]{3,2,0,1:T(8,128)(2,1)S(1)}, bf16[20,1,16,720]{3,2,0,1:T(8,128)(2,1)S(1)}, u32[]{:S(2)}, u32[]{:S(2)}) collective-permute-start(bf16[20,1,16,720]{3,2,0,1:T(8,128)(2,1)S(1)} %get-tuple-element.116), channel_id=1, source_target_pairs={{4,0},{8,4},{12,8},{16,12},{20,16},{24,20},{28,24},{32,28},{36,32}... | collective-permute-start | bytes 1382408 | tf_op jit(solution)/shard_map/ppermute | solution.py:18
  165.6 6.5 %collective-permute-done.2 = bf16[20,1,16,720]{3,2,0,1:T(8,128)(2,1)S(1)} collective-permute-done((bf16[20,1,16,720]{3,2,0,1:T(8,128)(2,1)S(1)}, bf16[20,1,16,720]{3,2,0,1:T(8,128)(2,1)S(1)}, u32[]{:S(2)}, u32[]{:S(2)}) %collective-permute-start.2) | collective-permute-done | bytes 460832 | tf_op jit(solution)/shard_map/ppermute | solution.py:15
  172.1 11.3 %fusion.31 = bf16[20,1,45,720]{3,2,0,1:T(8,128)(2,1)S(1)} fusion(bf16[20,1,16,720]{3,2,0,1:T(8,128)(2,1)S(1)} %collective-permute-done.3, bf16[20,1,45,720]{3,2,0,1:T(8,128)(2,1)S(1)} %fusion.13, bf16[20,1,16,720]{3,2,0,1:T(8,128)(2,1)S(1)} %collective-permute-done.2, f32[]{:T(128)} %bitcast.26, f32[]{:T(128)} %bitcast.25, f32[]{:T(128)} %bitcast.24, ...), kind=kOutput, calls=%fused_computation.45 | convolution fusion | flops 107279912 | bytes 3513668 | tf_op jit(solution)/shard_map/ij,mljk->mlik/dot_general | solution.py:47
  184.3 11.7 %fusion.24 = f32[20,45,5,144]{3,1,2,0:T(8,128)S(1)} fusion(f32[]{:T(128)} %bitcast.53, f32[]{:T(128)} %bitcast.52, f32[]{:T(128)} %bitcast.51, f32[]{:T(128)} %bitcast.50, f32[]{:T(128)} %bitcast.49, f32[]{:T(128)} %bitcast.48, f32[]{:T(128)} %bitcast.47, f32[]{:T(128)} %bitcast.46, f32[]{:T(128)} %bitcast.45, f32[]{:T(128)} %bitcast.44, f32[]{:T(128)} %bitcast.43, ...), kind=kOutput, calls=%fused_computation.38 | convolution fusion | flops 229439232 | bytes 4176772 | tf_op jit(solution)/shard_map/mlibk,kq->mlibq/dot_general | solution.py:60
  196.0 6.4 %copy.52 = f32[20,45,5,144]{3,2,1,0:T(8,128)} copy(f32[20,45,5,144]{3,1,2,0:T(8,128)S(1)} %fusion.24) | data formatting | bytes 5184000 | tf_op jit(solution)/shard_map/mlibk,kq->mlibq/dot_general | solution.py:60
  202.4 4.9 %reshape.122 = f32[20,1,45,720]{3,2,0,1:T(8,128)S(1)} reshape(f32[20,45,5,144]{3,2,1,0:T(8,128)} %copy.52) | data formatting | bytes 5184000 | tf_op jit(solution)/shard_map/reshape | solution.py:61
  207.3 1.7 convert_add_fusion
  208.9 4.4 %copy.53 = f32[20,1,45,720]{3,1,2,0:T(1,128)} copy(f32[20,1,45,720]{3,2,0,1:T(8,128)S(1)} %convert_add_fusion) | data formatting | bytes 5184000 | tf_op jit(solution)/shard_map/add | solution.py:153
  (83 shorter events, 23.7 us)
Async XLA Ops:
  6.5 45.3 %copy-start.1 = (bf16[20,1,45,720]{3,2,1,0:T(8,128)(2,1)S(1)}, bf16[20,1,45,720]{3,2,1,0:T(8,128)(2,1)}, u32[]{:S(2)}) copy-start(bf16[20,1,45,720]{3,2,1,0:T(8,128)(2,1)} %param.12) | copy-start | bytes 3888004
  8.0 43.7 %collective-permute-start = (bf16[20,1,16,720]{3,2,0,1:T(8,128)(2,1)S(1)}, bf16[20,1,16,720]{3,2,0,1:T(8,128)(2,1)}, u32[]{:S(2)}, u32[]{:S(2)}) collective-permute-start(bf16[20,1,16,720]{3,2,0,1:T(8,128)(2,1)S(1)} %get-tuple-element.117), channel_id=1, source_target_pairs={{0,4},{4,8},{8,12},{12,16},{16,20},{20,24},{24,28},{28,32},{32,36}... | collective-permute-start | bytes 1382408 | tf_op jit(solution)/shard_map/ppermute | solution.py:15
  8.1 43.6 %collective-permute-start.1 = (bf16[20,1,16,720]{3,2,0,1:T(8,128)(2,1)S(1)}, bf16[20,1,16,720]{3,2,0,1:T(8,128)(2,1)}, u32[]{:S(2)}, u32[]{:S(2)}) collective-permute-start(bf16[20,1,16,720]{3,2,0,1:T(8,128)(2,1)S(1)} %get-tuple-element.118), channel_id=1, source_target_pairs={{4,0},{8,4},{12,8},{16,12},{20,16},{24,20},{28,24},{32,28},{36,32}... | collective-permute-start | bytes 1382408 | tf_op jit(solution)/shard_map/ppermute | solution.py:18
  14.6 11.5 %all-to-all-start = ((s32[1,32,256]{2,0,1:T(1,128)}), s32[1,32,256]{2,0,1:T(1,128)S(1)}, u32[]{:S(2)}, u32[]{:S(2)}) async-start(s32[1,32,256]{2,0,1:T(1,128)} %copy.42), calls=%async_computation | async-start | bytes 65536 | tf_op jit(solution)/shard_map/all_to_all | solution.py:137
  26.1 14.3 %all-to-all-start.1 = ((f32[1,32,256]{2,0,1:T(1,128)}), f32[1,32,256]{2,0,1:T(1,128)S(1)}, u32[]{:S(2)}, u32[]{:S(2)}) async-start(f32[1,32,256]{2,0,1:T(1,128)} %compare_select_fusion), calls=%async_computation.1 | async-start | bytes 65536 | tf_op jit(solution)/shard_map/all_to_all | solution.py:136
  40.4 11.3 %all-to-all-start.2 = ((f32[1,32,256]{2,0,1:T(1,128)}), f32[1,32,256]{2,0,1:T(1,128)S(1)}, u32[]{:S(2)}, u32[]{:S(2)}) async-start(f32[1,32,256]{2,0,1:T(1,128)} %copy.50), calls=%async_computation.2 | async-start | bytes 65536 | tf_op jit(solution)/shard_map/all_to_all | solution.py:135
  44.2 86.5 %all-reduce.4.cloned.1.call-start = ((), (), s32[]{:S(2)}) async-start(), calls=%async_computation.3 | async-start | bytes 294912 | tf_op jit(solution)/shard_map/psum | solution.py:146
  131.9 28.1 %copy-start = (bf16[20,1,45,720]{3,2,1,0:T(8,128)(2,1)S(1)}, bf16[20,1,45,720]{3,2,1,0:T(8,128)(2,1)}, u32[]{:S(2)}) copy-start(bf16[20,1,45,720]{3,2,1,0:T(8,128)(2,1)} %param.13) | copy-start | bytes 3888004
  160.4 11.6 %collective-permute-start.2 = (bf16[20,1,16,720]{3,2,0,1:T(8,128)(2,1)S(1)}, bf16[20,1,16,720]{3,2,0,1:T(8,128)(2,1)S(1)}, u32[]{:S(2)}, u32[]{:S(2)}) collective-permute-start(bf16[20,1,16,720]{3,2,0,1:T(8,128)(2,1)S(1)} %get-tuple-element.115), channel_id=1, source_target_pairs={{0,4},{4,8},{8,12},{12,16},{16,20},{20,24},{24,28},{28,32},{32,36}... | collective-permute-start | bytes 1382408 | tf_op jit(solution)/shard_map/ppermute | solution.py:15
  160.5 11.6 %collective-permute-start.3 = (bf16[20,1,16,720]{3,2,0,1:T(8,128)(2,1)S(1)}, bf16[20,1,16,720]{3,2,0,1:T(8,128)(2,1)S(1)}, u32[]{:S(2)}, u32[]{:S(2)}) collective-permute-start(bf16[20,1,16,720]{3,2,0,1:T(8,128)(2,1)S(1)} %get-tuple-element.116), channel_id=1, source_target_pairs={{4,0},{8,4},{12,8},{16,12},{20,16},{24,20},{28,24},{32,28},{36,32}... | collective-permute-start | bytes 1382408 | tf_op jit(solution)/shard_map/ppermute | solution.py:18
Sparse Core Ops, SparseCore 0:
  90.7 40.0 all-reduce.3
where the time goes:
time: 222 us; the launch traced here: 220 us
  matrix products  73.5 us (33%)
  waiting for transfers between devices  61.3 us (28%)
  local copies, waits for them, and re-layouts  39.4 us (18%)
  starting transfers between devices  25.2 us (11%)
  between operations  13.7 us (6%)
  other arithmetic  6.39 us (3%)
    psum x1, waiting for transfers between devices, local(): increment = lax.psum(member_sum, 'mem')  40.2 us
    dot_general x2, matrix products, localize(): jnp.einsum('ij,mljk->mlik', band_lon, extended, preferred_element_type=jn...  23.7 us
    dot_general x2, matrix products, localize(): jnp.einsum('mlibk,kq->mlibq', windows, band_blocks, preferred_element_typ...  23.5 us
    dot_general x8, matrix products, pick_one_block(): jnp.dot(onehot_cols, field_cols, precision=lax.Precision.HIGHEST, preferr...  14.4 us
    dot_general x2, local copies, waits for them, and re-layouts, localize(): jnp.einsum('mlibk,kq->mlibq', windows, band_blocks, preferred_element_typ...  12.8 us
    dot_general x8, matrix products, spread_one_block(): jnp.dot(weighted.T, onehot_cols, precision=lax.Precision.HIGHEST, preferr...  11.9 us
    ppermute x2, starting transfers between devices, extended_2(): lax.ppermute(lax.slice_in_dim(block, 0, width, axis=dim), axis, backward)  10.1 us
    reshape x2, local copies, waits for them, and re-layouts, localize(): return result.reshape(members_here, levels, lon_cells, lat_cells)  9.75 us
  transfers between devices with their start and end apart: 8, of which 5 were waited for; matrix products, arithmetic and copies ran while one was open for 4% of the time, Pallas kernels for 0%

commit v1 on v0

v1 whole, which is shorter than its diff:
```python
import functools

import jax
import jax.numpy as jnp
from jax import lax
from jax.experimental import pallas as pl
from jax.experimental.pallas import tpu as pltpu
from jax.sharding import PartitionSpec as P

MESH = pl.DeviceIdType.MESH
F32 = jnp.float32
BF16 = jnp.bfloat16
SUM_TYPE = jnp.float32
GROUP = 5


def tap_columns(taps_ref):
    row = taps_ref[...].astype(F32).reshape(1, -1)
    return [row[:, d : d + 1] for d in range(row.shape[1])]


def band_of(distance, taps):
    band = jnp.zeros(distance.shape, F32)
    for d, tap in enumerate(taps):
        band = jnp.where(distance == d, tap, band)
    return band


def iota(shape, dim):
    return lax.broadcasted_iota(jnp.int32, shape, dim)


def build_bands(lon_ref, lat_ref, own_band, side_band, lat_band):
    lon_taps = tap_columns(lon_ref)
    lat_taps = tap_columns(lat_ref)
    rad = len(lon_taps) - 1
    shape = own_band.shape
    own_band[...] = band_of(jnp.abs(iota(shape, 0) - iota(shape, 1)), lon_taps).astype(BF16)
    shape = side_band.shape
    rows, cols = iota(shape, 0), iota(shape, 1)
    lon_cells = own_band.shape[1]
    place = jnp.where(cols < rad, cols - rad, cols - rad + lon_cells)
    side_band[...] = band_of(jnp.abs(rows - place), lon_taps).astype(BF16)
    width = lat_band.shape[1]

    def fill(i, carry):
        shape = (16, width)
        start = pl.multiple_of(i * 16, 16)
        away = jnp.abs(iota(shape, 0) + (start - 128) - iota(shape, 1))
        lat_band[pl.ds(start, 16), :] = band_of(away, lat_taps).astype(BF16)
        return carry

    lax.fori_loop(0, lat_band.shape[0] // 16, fill, 0)


def dot(a, b):
    return jnp.dot(a, b, preferred_element_type=F32)


def along_lat(field, band, out):
    lat = field.shape[1]
    out[:, 0:256] = dot(field[:, 0:384], band[128:512, :])
    out[:, 256:512] = dot(field[:, 128:640], band[0:512, :])
    out[:, 512:lat] = dot(field[:, 384:lat], band[0 : lat - 384, 0 : lat - 512])


def forward_kernel(
    tiles,
    groups,
    control,
    perturb,
    lon_taps,
    lat_taps,
    innov,
    inv_var,
    cell_index,
    counts,
    spread_own,
    spread_side,
    perturb_side,
    own_band,
    side_band,
    lat_band,
    control_own,
    perturb_own,
    control_low,
    perturb_low,
    control_side,
    along,
    smooth,
    total,
    send_sum,
    send_edge,
    got_sum,
    got_edge,
    lists,
    stage,
    got_lists,
    onehot,
    picked,
    places,
    field_parts,
    fields,
    field_edge,
    got_field,
    load_sem,
    halo_send,
    halo_recv,
    list_send,
    list_recv,
    sum_send,
    sum_recv,
    edge_send,
    edge_recv,
    field_send,
    field_recv,
):
    me = lax.axis_index("tile")
    mine = lax.axis_index("mem")
    mems = got_sum.shape[0] + 1
    members, lon_cells, lat = control_own.shape
    rad = control_side.shape[1] // 2
    cap = innov.shape[2]
    left, right = lax.rem(me + tiles - 1, tiles), lax.rem(me + 1, tiles)
    sides = (left, right)

    loads = [
        pltpu.make_async_copy(
            control.at[pl.ds(g * GROUP, GROUP), 0],
            control_own.at[pl.ds(g * GROUP, GROUP)],
            load_sem.at[g],
        )
        for g in range(groups)
    ]
    loads.append(pltpu.make_async_copy(perturb.at[:, 0], perturb_own, load_sem.at[groups]))
    loads.append(pltpu.make_async_copy(inv_var.at[0], lists.at[0], load_sem.at[groups + 1]))
    loads.append(pltpu.make_async_copy(innov.at[0], lists.at[1], load_sem.at[groups + 2]))
    for load in loads:
        load.start()

    partners = [(tile, mine) for tile in sides]
    partners += [(me, lax.rem(mine + j, mems)) for j in range(1, mems)]
    partners += [(tile, lax.rem(mine + j, mems)) for tile in sides for j in range(1, mems)]
    partners += [(lax.rem(me + i, tiles), mine) for i in range(2, tiles - 1)]
    barrier = pltpu.get_barrier_semaphore()
    for partner in partners:
        pl.semaphore_signal(barrier, inc=1, device_id=partner, device_id_type=MESH)

    def low_edge(own, low, start):
        for k in range(GROUP):
            field = own[start + k].astype(F32)
            low[start + k] = field[lon_cells - rad :, :].astype(BF16)

    for g in range(groups):
        loads[g].wait()
        low_edge(control_own, control_low, g * GROUP)

    def list_copy(i):
        return pltpu.make_async_remote_copy(
            stage.at[lax.rem(me + i, tiles)],
            got_lists.at[i],
            list_send.at[i],
            list_recv.at[i],
            device_id=(lax.rem(me + i, tiles), mine),
            device_id_type=MESH,
        )

    def halo_copies(own, low, side, kind, g):
        chunk = pl.ds(g * GROUP, GROUP)
        return (
            pltpu.make_async_remote_copy(
                own.at[chunk, 0:rad],
                side.at[chunk, rad : 2 * rad],
                halo_send.at[kind, 0, g],
                halo_recv.at[kind, 0, g],
                device_id=(left, mine),
                device_id_type=MESH,
            ),
            pltpu.make_async_remote_copy(
                low.at[chunk],
                side.at[chunk, 0:rad],
                halo_send.at[kind, 1, g],
                halo_recv.at[kind, 1, g],
                device_id=(right, mine),
                device_id_type=MESH,
            ),
        )

    def control_copies(g):
        return halo_copies(control_own, control_low, control_side, 0, g)

    def perturb_copies(g):
        return halo_copies(perturb_own, perturb_low, perturb_side, 1, g)

    pl.semaphore_wait(barrier, len(partners))
    for g in range(groups):
        for copy in control_copies(g):
            copy.start()

    for load in loads[groups:]:
        load.wait()
    shape = (tiles, tiles)
    count_row = counts[...].astype(F32)
    count_col = jnp.sum(
        jnp.where(iota(shape, 0) == iota(shape, 1), count_row, 0.0), axis=1, keepdims=True
    )
    live = iota((tiles, cap), 1).astype(F32) < count_col
    weight = jnp.where(live, lists[0], 0.0)
    stage[:, 0, 0:cap] = weight
    stage[:, 0, cap : 2 * cap] = weight * lists[1]
    stage[:, 0, 2 * cap : 3 * cap] = cell_index[0].astype(F32)
    for i in range(1, tiles):
        list_copy(i).start()
    got_lists[0] = stage[me]
    for g in range(groups):
        low_edge(perturb_own, perturb_low, g * GROUP)
    build_bands(lon_taps, lat_taps, own_band, side_band, lat_band)

    total[...] = jnp.zeros_like(total)
    rows = own_band.shape[0]

    def forward(g, carry):
        for copy in control_copies(g):
            copy.wait_recv()
        for copy in perturb_copies(g):
            copy.start()
        for k in range(GROUP):
            m = g * GROUP + k
            result = dot(own_band[...], control_own[m]) + dot(side_band[...], control_side[m])
            along[k * rows : (k + 1) * rows, :] = result.astype(BF16)
        along_lat(along, lat_band, smooth)
        running = total[...]
        for k in range(GROUP):
            m = g * GROUP + k
            running = running + perturb_own[m].astype(F32) * smooth[k * rows : k * rows + lon_cells, :]
        total[...] = running
        return carry

    lax.fori_loop(0, groups, forward, 0)

    result = total[...]
    send_sum[0:lon_cells, :] = result.astype(send_sum.dtype)
    send_edge[...] = result[lon_cells - rad :, :].astype(send_edge.dtype)
    sum_copies = []
    for j in range(1, mems):
        sum_copies.append(
            pltpu.make_async_remote_copy(
                send_sum,
                got_sum.at[j - 1],
                sum_send.at[j - 1],
                sum_recv.at[j - 1],
                device_id=(me, lax.rem(mine + j, mems)),
                device_id_type=MESH,
            )
        )
    for j in range(mems):
        for side in range(2):
            sum_copies.append(
                pltpu.make_async_remote_copy(
                    send_sum.at[0:rad] if side == 0 else send_edge,
                    got_edge.at[1 - side, j],
                    edge_send.at[side, j],
                    edge_recv.at[side, j],
                    device_id=(sides[side], lax.rem(mine + j, mems)),
                    device_id_type=MESH,
                )
            )
    for copy in sum_copies:
        copy.start()

    for i in range(1, tiles):
        list_copy(i).wait_recv()
    cells = got_lists[:, 0, 2 * cap : 3 * cap]
    row_of = jnp.floor((cells + 0.5) * (1.0 / lat))
    places[0] = row_of
    places[1] = cells - row_of * lat
    batch = onehot.shape[1] // cap
    field_parts[...] = jnp.zeros_like(field_parts)

    def scatter(s, carry):
        for k in range(batch):
            source = s * batch + k
            values = got_lists[source]
            rows_here = places[0, pl.ds(source, 1), :]
            cols_here = places[1, pl.ds(source, 1), :]
            lanes = slice(k * cap, (k + 1) * cap)
            hit = iota((rows, cap), 0).astype(F32) == rows_here
            for part in range(2):
                value = values[:, part * cap : (part + 1) * cap]
                high = value.astype(BF16).astype(F32)
                rest = value - high
                first = 2 * part * rows
                picked[first : first + rows, lanes] = jnp.where(hit, high, 0.0).astype(BF16)
                picked[first + rows : first + 2 * rows, lanes] = jnp.where(hit, rest, 0.0).astype(BF16)
            base = iota((16, cap), 0).astype(F32)
            for r in range(lat // 16):
                match = (base + float(16 * r)) == cols_here
                onehot[16 * r : 16 * r + 16, lanes] = jnp.where(match, 1.0, 0.0).astype(BF16)
        field_parts[...] += lax.dot_general(
            picked[...], onehot[...], (((1,), (1,)), ((), ())), preferred_element_type=F32
        )
        return carry

    lax.fori_loop(0, tiles // batch, scatter, 0)
    for part in range(2):
        first = 2 * part * rows
        field = field_parts[first : first + lon_cells, :] + field_parts[first + rows : first + rows + lon_cells, :]
        fields[part] = field
        field_edge[0, part] = field[0:rad, :]
        field_edge[1, part] = field[lon_cells - rad :, :]
    field_copies = [
        pltpu.make_async_remote_copy(
            field_edge.at[side],
            got_field.at[1 - side],
            field_send.at[side],
            field_recv.at[side],
            device_id=(sides[side], mine),
            device_id_type=MESH,
        )
        for side in range(2)
    ]
    for copy in field_copies:
        copy.start()

    for copy in sum_copies:
        copy.wait_recv()
    increment = send_sum[0:lon_cells, :].astype(F32)
    for j in range(mems - 1):
        increment = increment + got_sum[j, 0:lon_cells, :].astype(F32)
    spread_own[...] = fields[0] * increment - fields[1]
    for copy in field_copies:
        copy.wait_recv()
    for side in range(2):
        increment = got_edge[side, 0].astype(F32)
        for j in range(1, mems):
            increment = increment + got_edge[side, j].astype(F32)
        spread_side[side * rad : (side + 1) * rad, :] = got_field[side, 0] * increment - got_field[side, 1]

    def finish(g, carry):
        for copy in control_copies(g):
            copy.wait_send()
        for copy in perturb_copies(g):
            copy.wait()
        return carry

    lax.fori_loop(0, groups, finish, 0)
    for i in range(1, tiles):
        list_copy(i).wait_send()
    for copy in sum_copies + field_copies:
        copy.wait_send()


def backward_kernel(
    groups,
    control,
    perturb,
    spread_own,
    spread_side,
    perturb_side,
    own_band,
    side_band,
    lat_band,
    gradient,
    control_own,
    perturb_own,
    side_own,
    along,
    smooth,
    out,
    load_sem,
    out_sem,
):
    members, lon_cells, lat = control_own.shape
    rows = own_band.shape[0]

    def load(g):
        chunk = pl.ds(g * GROUP, GROUP)
        return (
            pltpu.make_async_copy(perturb.at[chunk, 0], perturb_own.at[chunk], load_sem.at[0, g]),
            pltpu.make_async_copy(perturb_side.at[chunk], side_own.at[chunk], load_sem.at[1, g]),
            pltpu.make_async_copy(control.at[chunk, 0], control_own.at[chunk], load_sem.at[2, g]),
        )

    def store(m):
        return pltpu.make_async_copy(out.at[m], gradient.at[m], out_sem.at[m])

    for g in range(groups):
        for copy in load(g):
            copy.start()

    def backward(g, carry):
        for copy in load(g):
            copy.wait()
        for k in range(GROUP):
            m = g * GROUP + k
            own = (perturb_own[m].astype(F32) * spread_own[...]).astype(BF16)
            side = (side_own[m].astype(F32) * spread_side[...]).astype(BF16)
            result = dot(own_band[...], own) + dot(side_band[...], side)
            along[k * rows : (k + 1) * rows, :] = result.astype(BF16)
        along_lat(along, lat_band, smooth)
        for k in range(GROUP):
            m = g * GROUP + k
            value = control_own[m].astype(F32) + smooth[k * rows : k * rows + lon_cells, :]
            out[m] = value[:, None, :]
            store(m).start()
        return carry

    lax.fori_loop(0, groups, backward, 0)

    def finish(m, carry):
        store(m).wait()
        return carry

    lax.fori_loop(0, members, finish, 0)


def local(tiles, mems, control, perturb, lon_taps, lat_taps, innov, inv_var, cell_index, counts):
    members, levels, lon_cells, lat = control.shape
    rad = lon_taps.shape[0] - 1
    cap = innov.shape[2]
    groups = members // GROUP
    rows = (lon_cells + 15) // 16 * 16
    dma = pltpu.SemaphoreType.DMA
    anywhere = pl.BlockSpec(memory_space=pl.ANY)
    inside = pl.BlockSpec(memory_space=pltpu.VMEM)
    batch = 4
    scratch = [
        pltpu.VMEM((members, lon_cells, lat), BF16),
        pltpu.VMEM((members, lon_cells, lat), BF16),
        pltpu.VMEM((members, rad, lat), BF16),
        pltpu.VMEM((members, rad, lat), BF16),
        pltpu.VMEM((members, 2 * rad, lat), BF16),
        pltpu.VMEM((GROUP * rows, lat), BF16),
        pltpu.VMEM((GROUP * rows, lat), F32),
        pltpu.VMEM((lon_cells, lat), F32),
        pltpu.VMEM((rows, lat), SUM_TYPE),
        pltpu.VMEM((rad, lat), SUM_TYPE),
        pltpu.VMEM((mems - 1, rows, lat), SUM_TYPE),
        pltpu.VMEM((2, mems, rad, lat), SUM_TYPE),
        pltpu.VMEM((2, tiles, cap), F32),
        pltpu.VMEM((tiles, 1, 3 * cap), F32),
        pltpu.VMEM((tiles, 1, 3 * cap), F32),
        pltpu.VMEM((lat, batch * cap), BF16),
        pltpu.VMEM((4 * rows, batch * cap), BF16),
        pltpu.VMEM((2, tiles, cap), F32),
        pltpu.VMEM((4 * rows, lat), F32),
        pltpu.VMEM((2, lon_cells, lat), F32),
        pltpu.VMEM((2, 2, rad, lat), F32),
        pltpu.VMEM((2, 2, rad, lat), F32),
        dma((groups + 3,)),
        dma((2, 2, groups)),
        dma((2, 2, groups)),
        dma((tiles,)),
        dma((tiles,)),
        dma((mems - 1,)),
        dma((mems - 1,)),
        dma((2, mems)),
        dma((2, mems)),
        dma((2,)),
        dma((2,)),
    ]
    spread_own, spread_side, perturb_side, own_band, side_band, lat_band = pl.pallas_call(
        functools.partial(forward_kernel, tiles, groups),
        out_shape=(
            jax.ShapeDtypeStruct((lon_cells, lat), F32),
            jax.ShapeDtypeStruct((2 * rad, lat), F32),
            jax.ShapeDtypeStruct((members, 2 * rad, lat), BF16),
            jax.ShapeDtypeStruct((rows, lon_cells), BF16),
            jax.ShapeDtypeStruct((rows, 2 * rad), BF16),
            jax.ShapeDtypeStruct((512, 256), BF16),
        ),
        in_specs=[anywhere, anywhere, inside, inside, anywhere, anywhere, inside, inside],
        out_specs=(inside, inside, anywhere, inside, inside, inside),
        scratch_shapes=scratch,
        compiler_params=pltpu.CompilerParams(
            collective_id=0, has_side_effects=True, vmem_limit_bytes=48 * 2**20
        ),
        name="forward",
    )(control, perturb, lon_taps, lat_taps, innov, inv_var, cell_index, counts)
    gradient = pl.pallas_call(
        functools.partial(backward_kernel, groups),
        out_shape=jax.ShapeDtypeStruct((members, lon_cells, 1, lat), F32),
        in_specs=[anywhere, anywhere, inside, inside, anywhere, inside, inside, inside],
        out_specs=anywhere,
        scratch_shapes=[
            pltpu.VMEM((members, lon_cells, lat), BF16),
            pltpu.VMEM((members, lon_cells, lat), BF16),
            pltpu.VMEM((members, 2 * rad, lat), BF16),
            pltpu.VMEM((GROUP * rows, lat), BF16),
            pltpu.VMEM((GROUP * rows, lat), F32),
            pltpu.VMEM((members, lon_cells, 1, lat), F32),
            dma((3, groups)),
            dma((members,)),
        ],
        compiler_params=pltpu.CompilerParams(vmem_limit_bytes=48 * 2**20),
        name="backward",
    )(control, perturb, spread_own, spread_side, perturb_side, own_band, side_band, lat_band)
    return gradient.reshape(members, levels, lon_cells, lat)


def solution(mesh):
    return jax.shard_map(
        functools.partial(local, mesh.shape["tile"], mesh.shape["mem"]),
        mesh=mesh,
        in_specs=(
            P("mem", None, "tile", None),
            P("mem", None, "tile", None),
            P(),
            P(),
            P("tile", None, None),
            P("tile", None, None),
            P("tile", None, None),
            P("tile", None),
        ),
        out_specs=P("mem", None, "tile", None),
        check_vma=False,
    )
```

time: 222 us -> 47.2 us (0.21)
  the two profiles are of different devices: /device:TPU:0 before, /device:TPU:1 now
where the time goes in v1:
time: 47.2 us; the launch traced here: 46.8 us
  Pallas kernels  39.8 us (84%)
  local copies, waits for them, and re-layouts  6.98 us (15%)
    pallas_call x1, Pallas kernels, local(): pl.pallas_call(functools.partial(forward_kernel, tiles, groups), out_shap...  33.4 us
    unnamed x16, local copies, waits for them, and re-layouts  6.98 us
    pallas_call x1, Pallas kernels, local(): pl.pallas_call(functools.partial(backward_kernel, groups), out_shape=jax....  6.35 us

profile of v1, /device:TPU:1, one launch (start us, length us, event | category | flops | bytes accessed | tf_op | source)
XLA Modules:
  0.0 46.8 jit_solution(8966791063847115273)
XLA Ops:
  0.0 0.0 copy-start
  0.0 1.4 %copy-done = bf16[20,1,45,720]{3,2,1,0:T(8,128)(2,1)S(1)} copy-done((bf16[20,1,45,720]{3,2,1,0:T(8,128)(2,1)S(1)}, bf16[20,1,45,720]{3,2,1,0:T(8,128)(2,1)}, u32[]{:S(2)}) %copy-start) | copy-done | bytes 1296024
  1.4 0.0 copy-start.1
  1.4 1.4 %copy-done.1 = bf16[20,1,45,720]{3,2,1,0:T(8,128)(2,1)S(1)} copy-done((bf16[20,1,45,720]{3,2,1,0:T(8,128)(2,1)S(1)}, bf16[20,1,45,720]{3,2,1,0:T(8,128)(2,1)}, u32[]{:S(2)}) %copy-start.1) | copy-done | bytes 1296024
  2.7 0.0 copy-start.2
  2.8 0.8 %copy-done.2 = f32[1,32,256]{2,1,0:T(8,128)S(1)} copy-done((f32[1,32,256]{2,1,0:T(8,128)S(1)}, f32[1,32,256]{2,1,0:T(8,128)}, u32[]{:S(2)}) %copy-start.2) | copy-done | bytes 32792
  3.5 0.0 copy-start.3
  3.5 0.8 %copy-done.3 = f32[1,32,256]{2,1,0:T(8,128)S(1)} copy-done((f32[1,32,256]{2,1,0:T(8,128)S(1)}, f32[1,32,256]{2,1,0:T(8,128)}, u32[]{:S(2)}) %copy-start.3) | copy-done | bytes 32792
  4.3 0.0 copy-start.4
  4.3 0.8 %copy-done.4 = s32[1,32,256]{2,1,0:T(8,128)S(1)} copy-done((s32[1,32,256]{2,1,0:T(8,128)S(1)}, s32[1,32,256]{2,1,0:T(8,128)}, u32[]{:S(2)}) %copy-start.4) | copy-done | bytes 32792
  5.0 0.0 copy-start.5
  5.0 0.7 %copy-done.5 = bf16[17]{0:T(256)(128)(2,1)S(1)} copy-done((bf16[17]{0:T(256)(128)(2,1)S(1)}, bf16[17]{0:T(256)(128)(2,1)}, u32[]{:S(2)}) %copy-start.5) | copy-done | bytes 58
  5.7 0.0 copy-start.6
  5.7 0.7 %copy-done.6 = bf16[17]{0:T(256)(128)(2,1)S(1)} copy-done((bf16[17]{0:T(256)(128)(2,1)S(1)}, bf16[17]{0:T(256)(128)(2,1)}, u32[]{:S(2)}) %copy-start.6) | copy-done | bytes 58
  6.3 0.0 copy-start.7
  6.3 0.7 %copy-done.7 = s32[1,32]{1,0:T(1,128)S(1)} copy-done((s32[1,32]{1,0:T(1,128)S(1)}, s32[1,32]{1,0:T(1,128)}, u32[]{:S(2)}) %copy-start.7) | copy-done | bytes 152
  7.0 33.4 %forward.1 = (f32[45,720]{1,0:T(8,128)S(1)}, f32[32,720]{1,0:T(8,128)S(1)}, bf16[20,32,720]{2,1,0:T(8,128)(2,1)S(1)}, bf16[48,45]{1,0:T(8,128)(2,1)S(1)}, bf16[4...) custom-call(bf16[20,1,45,720]{3,2,1,0:T(8,128)(2,1)S(1)} %copy-done, bf16[20,1,45,720]{3,2,1,0:T(8,128)(2,1)S(1)} %copy-done.1, ...), custom_call_target="tpu_custom_call" | custom-call | tf_op jit(solution)/shard_map/forward/pallas_call | solution.py:462
  40.4 6.3 %backward.1 = f32[20,45,1,720]{3,2,1,0:T(1,128)} custom-call(bf16[20,1,45,720]{3,2,1,0:T(8,128)(2,1)S(1)} %copy-done, bf16[20,1,45,720]{3,2,1,0:T(8,128)(2,1)S(1)} %copy-done.1, f32[45,720]{1,0:T(8,128)S(1)} %get-tuple-element.11.spread_own, f32[32,720]{1,0:T(8,128)S(1)} %get-tuple-element.12.spread_side, ...), custom_call_target="tpu_custom_call" | custom-call | tf_op jit(solution)/shard_map/backward/pallas_call | solution.py:480
Async XLA Ops:
  0.0 1.4 %copy-start = (bf16[20,1,45,720]{3,2,1,0:T(8,128)(2,1)S(1)}, bf16[20,1,45,720]{3,2,1,0:T(8,128)(2,1)}, u32[]{:S(2)}) copy-start(bf16[20,1,45,720]{3,2,1,0:T(8,128)(2,1)} %control.3) | copy-start | bytes 3888004
  1.4 1.4 %copy-start.1 = (bf16[20,1,45,720]{3,2,1,0:T(8,128)(2,1)S(1)}, bf16[20,1,45,720]{3,2,1,0:T(8,128)(2,1)}, u32[]{:S(2)}) copy-start(bf16[20,1,45,720]{3,2,1,0:T(8,128)(2,1)} %perturb.3) | copy-start | bytes 3888004
  2.7 0.8 %copy-start.2 = (f32[1,32,256]{2,1,0:T(8,128)S(1)}, f32[1,32,256]{2,1,0:T(8,128)}, u32[]{:S(2)}) copy-start(f32[1,32,256]{2,1,0:T(8,128)} %innov.1) | copy-start | bytes 98308
  3.5 0.8 %copy-start.3 = (f32[1,32,256]{2,1,0:T(8,128)S(1)}, f32[1,32,256]{2,1,0:T(8,128)}, u32[]{:S(2)}) copy-start(f32[1,32,256]{2,1,0:T(8,128)} %inv_var.1) | copy-start | bytes 98308
  4.3 0.8 %copy-start.4 = (s32[1,32,256]{2,1,0:T(8,128)S(1)}, s32[1,32,256]{2,1,0:T(8,128)}, u32[]{:S(2)}) copy-start(s32[1,32,256]{2,1,0:T(8,128)} %cell_index.1) | copy-start | bytes 98308
  5.0 0.7 %copy-start.5 = (bf16[17]{0:T(256)(128)(2,1)S(1)}, bf16[17]{0:T(256)(128)(2,1)}, u32[]{:S(2)}) copy-start(bf16[17]{0:T(256)(128)(2,1)} %lon_taps.1) | copy-start | bytes 106
  5.7 0.7 %copy-start.6 = (bf16[17]{0:T(256)(128)(2,1)S(1)}, bf16[17]{0:T(256)(128)(2,1)}, u32[]{:S(2)}) copy-start(bf16[17]{0:T(256)(128)(2,1)} %lat_taps.1) | copy-start | bytes 106
  6.3 0.7 %copy-start.7 = (s32[1,32]{1,0:T(1,128)S(1)}, s32[1,32]{1,0:T(1,128)}, u32[]{:S(2)}) copy-start(s32[1,32]{1,0:T(1,128)} %counts.1) | copy-start | bytes 388

commit v2 on v1

v2 whole, which is shorter than its diff:
```python
import functools

import jax
import jax.numpy as jnp
from jax import lax
from jax.experimental import pallas as pl
from jax.experimental.pallas import tpu as pltpu
from jax.sharding import PartitionSpec as P

MESH = pl.DeviceIdType.MESH
F32 = jnp.float32
BF16 = jnp.bfloat16
GROUP = 5
BACK = 5
AHEAD = 2
PART = 256


def iota(shape, dim):
    return lax.broadcasted_iota(jnp.int32, shape, dim)


def band_block(taps_ref):
    row = taps_ref[...].astype(F32).reshape(1, -1)
    taps = [jnp.broadcast_to(row[:, d : d + 1], (16, 128)) for d in range(row.shape[1])]

    def block(offsets):
        away = jnp.abs(offsets)
        band = jnp.zeros((16, 128), F32)
        for d, tap in enumerate(taps):
            band = jnp.where(away == d, tap, band)
        return band.astype(BF16)

    return block


def build_bands(lon_ref, lat_ref, lon_band, lat_band, lon_cells):
    rad = lon_ref.shape[0] - 1
    rows, depth = lon_band.shape
    row, col = iota((16, 128), 0), iota((16, 128), 1)
    block = band_block(lon_ref)
    side = col - rows
    place = jnp.where(side < rad, side - rad, side - rad + lon_cells)
    place = jnp.where(side < 0, jnp.where(col < lon_cells, col, 4 * rows), place)
    for r in range(0, rows, 16):
        lon_band[r : r + 16, :] = block(row + r - place)[:, 0:depth]
    block = band_block(lat_ref)
    lat_band[...] = jnp.zeros_like(lat_band)
    for r in range(-16, 144, 16):
        piece = block(row + r - col)
        for half in range(2):
            first = 128 + 128 * half + r
            lat_band[first : first + 16, 128 * half : 128 * half + 128] = piece


def dot(a, b):
    return jnp.dot(a, b, preferred_element_type=F32)


def along_lat(along, band):
    windows = [along[:, PART * n : PART * n + 512] for n in range(along.shape[1] // PART - 1)]
    return dot(jnp.concatenate(windows, axis=0), band[...])


def forward_kernel(
    tiles,
    mems,
    groups,
    control,
    perturb,
    lon_taps,
    lat_taps,
    innov,
    inv_var,
    cell_index,
    counts,
    spread,
    perturb_wide,
    lon_band_out,
    lat_band_out,
    lon_band,
    lat_band,
    control_own,
    perturb_own,
    control_low,
    perturb_low,
    control_wide,
    perturb_full,
    along,
    total,
    got_sum,
    part,
    part_low,
    lists,
    cells_here,
    counts_here,
    lon_here,
    lat_here,
    stage,
    got_lists,
    onehot,
    picked,
    places,
    field_parts,
    load_sem,
    keep_sem,
    halo_send,
    halo_recv,
    list_send,
    list_recv,
    sum_send,
    sum_recv,
    part_send,
    part_recv,
    edge_send,
    edge_recv,
):
    me = lax.axis_index("tile")
    mine = lax.axis_index("mem")
    members, lon_cells, lat = control_own.shape
    rows, depth = lon_band.shape
    rad = (depth - rows) // 2
    cap = innov.shape[2]
    upper, lower = slice(rows, rows + rad), slice(rows + rad, depth)
    parts = total.shape[1] // PART
    left, right = lax.rem(me + tiles - 1, tiles), lax.rem(me + 1, tiles)
    sides = (left, right)
    turn = lax.rem(me, 2) * (mems // 2)
    rank = lax.rem(mine + turn, mems)

    loads = [
        pltpu.make_async_copy(
            control.at[pl.ds(g * GROUP, GROUP), 0],
            control_own.at[pl.ds(g * GROUP, GROUP)],
            load_sem.at[g],
        )
        for g in range(groups)
    ]
    others = (
        (inv_var.at[0], lists.at[0]),
        (innov.at[0], lists.at[1]),
        (cell_index.at[0], cells_here),
        (counts, counts_here),
        (perturb.at[:, 0], perturb_own),
        (lon_taps, lon_here),
        (lat_taps, lat_here),
    )
    loads += [
        pltpu.make_async_copy(src, dst, load_sem.at[groups + n]) for n, (src, dst) in enumerate(others)
    ]
    late = groups + 4

    partners = [(tile, mine) for tile in sides]
    partners += [(me, lax.rem(mine + j, mems)) for j in range(1, mems)]
    partners += [(tile, lax.rem(mine + j, mems)) for tile in sides for j in range(1, mems)]
    partners += [(lax.rem(me + i, tiles), mine) for i in range(2, tiles - 1)]
    barrier = pltpu.get_barrier_semaphore()
    for partner in partners:
        pl.semaphore_signal(barrier, inc=1, device_id=partner, device_id_type=MESH)
    for n, load in enumerate(loads):
        if n != late:
            load.start()

    filler = jnp.zeros((rows - lon_cells, lat), F32)

    def stage_edges(own, low, full, start):
        for k in range(GROUP):
            field = own[start + k].astype(F32)
            low[start + k] = field[lon_cells - rad :, :].astype(BF16)
            full[start + k, 0:rows, :] = jnp.concatenate([field, filler], axis=0).astype(BF16)

    def list_copy(i):
        return pltpu.make_async_remote_copy(
            stage.at[lax.rem(me + i, tiles)],
            got_lists.at[i],
            list_send.at[i],
            list_recv.at[i],
            device_id=(lax.rem(me + i, tiles), mine),
            device_id_type=MESH,
        )

    def halo_copies(source, low, wide, kind, g):
        chunk = pl.ds(g * GROUP, GROUP)
        return (
            pltpu.make_async_remote_copy(
                source.at[chunk, 0:rad],
                wide.at[chunk, lower],
                halo_send.at[kind, 0, g],
                halo_recv.at[kind, 0, g],
                device_id=(left, mine),
                device_id_type=MESH,
            ),
            pltpu.make_async_remote_copy(
                low.at[chunk],
                wide.at[chunk, upper],
                halo_send.at[kind, 1, g],
                halo_recv.at[kind, 1, g],
                device_id=(right, mine),
                device_id_type=MESH,
            ),
        )

    def control_copies(g):
        return halo_copies(control_own, control_low, control_wide, 0, g)

    def perturb_copies(g):
        return halo_copies(perturb_own, perturb_low, perturb_wide, 1, g)

    loads[0].wait()
    stage_edges(control_own, control_low, control_wide, 0)
    pl.semaphore_wait(barrier, len(partners))
    for g in range(groups):
        if g > 0:
            loads[g].wait()
            stage_edges(control_own, control_low, control_wide, g * GROUP)
        for copy in control_copies(g):
            copy.start()

    loads[late].start()
    for n, load in enumerate(loads[groups:]):
        if groups + n != late:
            load.wait()
    shape = (tiles, tiles)
    count_row = counts_here[...].astype(F32)
    count_col = jnp.sum(
        jnp.where(iota(shape, 0) == iota(shape, 1), count_row, 0.0), axis=1, keepdims=True
    )
    live = iota((tiles, cap), 1).astype(F32) < count_col
    weight = jnp.where(live, lists[0], 0.0)
    stage[:, 0, 0:cap] = weight
    stage[:, 0, cap : 2 * cap] = weight * lists[1]
    stage[:, 0, 2 * cap : 3 * cap] = cells_here[...].astype(F32)
    for i in range(1, tiles):
        list_copy(i).start()
    got_lists[0] = stage[me]
    loads[late].wait()
    for g in range(groups):
        stage_edges(perturb_own, perturb_low, perturb_full, g * GROUP)
    build_bands(lon_here, lat_here, lon_band, lat_band, lon_cells)
    keeps = [
        pltpu.make_async_copy(src, dst, keep_sem.at[n])
        for n, (src, dst) in enumerate(
            (
                (lon_band, lon_band_out),
                (lat_band, lat_band_out),
                (perturb_full, perturb_wide.at[:, 0:rows]),
            )
        )
    ]
    for keep in keeps:
        keep.start()
    total[...] = jnp.zeros_like(total)
    along[...] = jnp.zeros_like(along)

    def forward(g, carry):
        for copy in control_copies(g):
            copy.wait_recv()
        for copy in perturb_copies(g):
            copy.start()
        for k in range(GROUP):
            result = dot(lon_band[...], control_wide[g * GROUP + k])
            along[k * rows : (k + 1) * rows, 128 : 128 + lat] = result.astype(BF16)
        smooth = along_lat(along, lat_band)
        for n in range(parts):
            lanes = slice(n * PART, min(lat, (n + 1) * PART))
            count = lanes.stop - lanes.start
            running = total[0:lon_cells, lanes]
            for k in range(GROUP):
                first = (n * GROUP + k) * rows
                weight = perturb_own[g * GROUP + k, :, lanes].astype(F32)
                running = running + weight * smooth[first : first + lon_cells, 0:count]
            total[0:lon_cells, lanes] = running
        return carry

    lax.fori_loop(0, groups, forward, 0)

    def lanes_of(q):
        return pl.ds(pl.multiple_of(jnp.minimum(q, parts - 1) * PART, PART), PART)

    def sum_copy(j):
        return pltpu.make_async_remote_copy(
            total.at[:, lanes_of(lax.rem(rank + j, mems))],
            got_sum.at[j - 1],
            sum_send.at[j - 1],
            sum_recv.at[j - 1],
            device_id=(me, lax.rem(mine + j, mems)),
            device_id_type=MESH,
        )

    def if_owner(owner, action):
        @pl.when(owner < parts)
        def _():
            action()

    for j in range(1, mems):
        if_owner(lax.rem(rank + j, mems), sum_copy(j).start)

    for i in range(1, tiles):
        list_copy(i).wait_recv()
    cells = got_lists[:, 0, 2 * cap : 3 * cap]
    row_of = jnp.floor((cells + 0.5) * (1.0 / lat))
    col_of = cells - row_of * lat - rank.astype(F32) * PART
    places[0] = row_of
    places[1] = jnp.where((col_of >= 0) & (col_of < PART), col_of, -1.0)
    batch = onehot.shape[1] // cap
    field_parts[...] = jnp.zeros_like(field_parts)
    row_base = iota((16, cap), 0).astype(F32).astype(BF16)
    one = jnp.ones((16, cap), BF16)
    nothing = jnp.zeros((16, cap), BF16)

    def wide(row):
        return jnp.broadcast_to(row, (16, cap)).astype(BF16)

    def scatter(s, carry):
        for k in range(batch):
            source = s * batch + k
            values = got_lists[source]
            lanes = slice(k * cap, (k + 1) * cap)
            row_at = wide(places[0, pl.ds(source, 1), :])
            col_at = wide(places[1, pl.ds(source, 1), :])
            for kind in range(2):
                value = values[:, kind * cap : (kind + 1) * cap]
                rest = wide(value - value.astype(BF16).astype(F32))
                high = wide(value)
                first = 2 * kind * rows
                for r in range(0, rows, 16):
                    match = row_base == row_at - r
                    picked[first + r : first + r + 16, lanes] = jnp.where(match, high, nothing)
                    picked[first + rows + r : first + rows + r + 16, lanes] = jnp.where(match, rest, nothing)
            for r in range(0, PART, 16):
                match = row_base == col_at - r
                onehot[r : r + 16, lanes] = jnp.where(match, one, nothing)
        field_parts[...] += lax.dot_general(
            picked[...], onehot[...], (((1,), (1,)), ((), ())), preferred_element_type=F32
        )
        return carry

    lax.fori_loop(0, tiles // batch, scatter, 0)
    fields = [
        field_parts[2 * kind * rows : (2 * kind + 1) * rows, :]
        + field_parts[(2 * kind + 1) * rows : (2 * kind + 2) * rows, :]
        for kind in range(2)
    ]

    def part_copy(j):
        return pltpu.make_async_remote_copy(
            part,
            spread.at[0:rows, lanes_of(rank)],
            part_send.at[j - 1],
            part_recv.at[rank],
            device_id=(me, lax.rem(mine + j, mems)),
            device_id_type=MESH,
        )

    def edge_copy(side, j):
        return pltpu.make_async_remote_copy(
            part.at[0:rad] if side == 0 else part_low,
            spread.at[lower if side == 0 else upper, lanes_of(rank)],
            edge_send.at[side, j],
            edge_recv.at[side, rank],
            device_id=(sides[side], lax.rem(mine + j, mems)),
            device_id_type=MESH,
        )

    def own_copy():
        return pltpu.make_async_copy(part, spread.at[0:rows, lanes_of(rank)], keep_sem.at[len(keeps)])

    @pl.when(rank < parts)
    def _():
        for j in range(1, mems):
            sum_copy(j).wait_recv()
        increment = total[:, lanes_of(rank)]
        for j in range(mems - 1):
            increment = increment + got_sum[j]
        result = fields[0] * increment - fields[1]
        part[...] = result
        part_low[...] = result[lon_cells - rad : lon_cells, :]
        for j in range(1, mems):
            edge_copy(0, j).start()
            edge_copy(1, j).start()
        for j in range(1, mems):
            part_copy(j).start()
        edge_copy(0, 0).start()
        edge_copy(1, 0).start()
        own_copy().start()

    def finish(g, carry):
        for copy in control_copies(g):
            copy.wait_send()
        for copy in perturb_copies(g):
            copy.wait()
        return carry

    lax.fori_loop(0, groups, finish, 0)
    for i in range(1, tiles):
        list_copy(i).wait_send()
    for keep in keeps:
        keep.wait()
    for j in range(1, mems):
        if_owner(lax.rem(rank + j, mems), sum_copy(j).wait_send)

    def got_part(p):
        return pltpu.make_async_remote_copy(
            part,
            spread.at[0:rows, p * PART : (p + 1) * PART],
            part_send.at[0],
            part_recv.at[p],
            device_id=(me, lax.rem(mine + 1, mems)),
            device_id_type=MESH,
        )

    def got_edge(side, p):
        return pltpu.make_async_remote_copy(
            part_low,
            spread.at[lower if side == 0 else upper, p * PART : (p + 1) * PART],
            edge_send.at[side, 0],
            edge_recv.at[side, p],
            device_id=(sides[side], mine),
            device_id_type=MESH,
        )

    for p in range(parts):

        @pl.when(rank != p)
        def _(p=p):
            got_part(p).wait_recv()

        for side in range(2):
            got_edge(side, p).wait_recv()

    @pl.when(rank < parts)
    def _():
        own_copy().wait()
        for j in range(1, mems):
            part_copy(j).wait_send()
        for j in range(mems):
            for side in range(2):
                edge_copy(side, j).wait_send()


def backward_kernel(
    groups,
    control,
    spread_in,
    perturb_wide,
    lon_band_in,
    lat_band_in,
    gradient,
    control_own,
    perturb_own,
    spread,
    lon_band,
    lat_band,
    along,
    out,
    first_sem,
    load_sem,
    out_sem,
):
    members, lon_cells, lat = control_own.shape
    rows = lon_band.shape[0]
    parts = spread.shape[1] // PART

    def load(g):
        chunk = pl.ds(g * BACK, BACK)
        return (
            pltpu.make_async_copy(perturb_wide.at[chunk], perturb_own.at[chunk], load_sem.at[0, g]),
            pltpu.make_async_copy(control.at[chunk, 0], control_own.at[chunk], load_sem.at[1, g]),
        )

    def store(m):
        return pltpu.make_async_copy(out.at[m], gradient.at[m], out_sem.at[m])

    pairs = ((spread_in, spread), (lon_band_in, lon_band), (lat_band_in, lat_band))
    firsts = [pltpu.make_async_copy(src, dst, first_sem.at[n]) for n, (src, dst) in enumerate(pairs)]
    load(0)[0].start()
    for copy in firsts:
        copy.start()
    load(0)[1].start()
    for g in range(1, AHEAD):
        for copy in load(g):
            copy.start()
    along[...] = jnp.zeros_like(along)
    for copy in firsts:
        copy.wait()

    def backward(g, carry):
        for copy in load(g):
            copy.wait()

        @pl.when(g + AHEAD < groups)
        def _():
            for copy in load(g + AHEAD):
                copy.start()

        for k in range(BACK):
            product = (perturb_own[g * BACK + k].astype(F32) * spread[:, 0:lat]).astype(BF16)
            result = dot(lon_band[...], product)
            along[k * rows : (k + 1) * rows, 128 : 128 + lat] = result.astype(BF16)
        smooth = along_lat(along, lat_band)
        for k in range(BACK):
            m = g * BACK + k
            for n in range(parts):
                lanes = slice(n * PART, min(lat, (n + 1) * PART))
                count = lanes.stop - lanes.start
                first = (n * BACK + k) * rows
                value = control_own[m, :, lanes].astype(F32) + smooth[first : first + lon_cells, 0:count]
                out[m, :, :, lanes] = value[:, None, :]
            store(m).start()
        return carry

    lax.fori_loop(0, groups, backward, 0)

    def finish(m, carry):
        store(m).wait()
        return carry

    lax.fori_loop(0, members, finish, 0)


def local(tiles, mems, control, perturb, lon_taps, lat_taps, innov, inv_var, cell_index, counts):
    members, levels, lon_cells, lat = control.shape
    rad = lon_taps.shape[0] - 1
    cap = innov.shape[2]
    groups = members // GROUP
    rows = (lon_cells + 15) // 16 * 16
    dma = pltpu.SemaphoreType.DMA
    anywhere = pl.BlockSpec(memory_space=pl.ANY)
    batch = 4
    width = (lat + PART - 1) // PART * PART
    depth = rows + 2 * rad
    bands = [pltpu.VMEM((rows, depth), BF16), pltpu.VMEM((512, PART), BF16)]
    scratch = bands + [
        pltpu.VMEM((members, lon_cells, lat), BF16),
        pltpu.VMEM((members, lon_cells, lat), BF16),
        pltpu.VMEM((members, rad, lat), BF16),
        pltpu.VMEM((members, rad, lat), BF16),
        pltpu.VMEM((members, depth, lat), BF16),
        pltpu.VMEM((members, rows, lat), BF16),
        pltpu.VMEM((GROUP * rows, width + PART), BF16),
        pltpu.VMEM((rows, width), F32),
        pltpu.VMEM((mems - 1, rows, PART), F32),
        pltpu.VMEM((rows, PART), F32),
        pltpu.VMEM((rad, PART), F32),
        pltpu.VMEM((2, tiles, cap), F32),
        pltpu.VMEM((tiles, cap), jnp.int32),
        pltpu.VMEM(counts.shape, jnp.int32),
        pltpu.VMEM(lon_taps.shape, BF16),
        pltpu.VMEM(lat_taps.shape, BF16),
        pltpu.VMEM((tiles, 1, 3 * cap), F32),
        pltpu.VMEM((tiles, 1, 3 * cap), F32),
        pltpu.VMEM((PART, batch * cap), BF16),
        pltpu.VMEM((4 * rows, batch * cap), BF16),
        pltpu.VMEM((2, tiles, cap), F32),
        pltpu.VMEM((4 * rows, PART), F32),
        dma((groups + 7,)),
        dma((4,)),
        dma((2, 2, groups)),
        dma((2, 2, groups)),
        dma((tiles,)),
        dma((tiles,)),
        dma((mems - 1,)),
        dma((mems - 1,)),
        dma((mems - 1,)),
        dma((mems,)),
        dma((2, mems)),
        dma((2, mems)),
    ]
    middle = pl.pallas_call(
        functools.partial(forward_kernel, tiles, mems, groups),
        out_shape=(
            jax.ShapeDtypeStruct((depth, width), F32),
            jax.ShapeDtypeStruct((members, depth, lat), BF16),
            jax.ShapeDtypeStruct((rows, depth), BF16),
            jax.ShapeDtypeStruct((512, PART), BF16),
        ),
        in_specs=[anywhere] * 8,
        out_specs=(anywhere,) * 4,
        scratch_shapes=scratch,
        compiler_params=pltpu.CompilerParams(
            collective_id=0, has_side_effects=True, vmem_limit_bytes=63 * 2**20
        ),
        name="forward",
    )(control, perturb, lon_taps, lat_taps, innov, inv_var, cell_index, counts)
    gradient = pl.pallas_call(
        functools.partial(backward_kernel, members // BACK),
        out_shape=jax.ShapeDtypeStruct((members, lon_cells, 1, lat), F32),
        in_specs=[anywhere] * 5,
        out_specs=anywhere,
        scratch_shapes=[
            pltpu.VMEM((members, lon_cells, lat), BF16),
            pltpu.VMEM((members, depth, lat), BF16),
            pltpu.VMEM((depth, width), F32),
            *bands,
            pltpu.VMEM((BACK * rows, width + PART), BF16),
            pltpu.VMEM((members, lon_cells, 1, lat), F32),
            dma((3,)),
            dma((2, members // BACK)),
            dma((members,)),
        ],
        compiler_params=pltpu.CompilerParams(vmem_limit_bytes=63 * 2**20),
        name="backward",
    )(control, *middle)
    return gradient.reshape(members, levels, lon_cells, lat)


def solution(mesh):
    return jax.shard_map(
        functools.partial(local, mesh.shape["tile"], mesh.shape["mem"]),
        mesh=mesh,
        in_specs=(
            P("mem", None, "tile", None),
            P("mem", None, "tile", None),
            P(),
            P(),
            P("tile", None, None),
            P("tile", None, None),
            P("tile", None, None),
            P("tile", None),
        ),
        out_specs=P("mem", None, "tile", None),
        check_vma=False,
    )
```

time: 47.2 us -> 33.5 us (0.71)
  the two profiles are of different devices: /device:TPU:1 before, /device:TPU:0 now
where the time goes in v2:
time: 33.5 us; the launch traced here: 33.3 us
  Pallas kernels  33.3 us (99%)
    pallas_call x1, Pallas kernels, local(): pl.pallas_call(functools.partial(forward_kernel, tiles, mems, groups), ou...  28.1 us
    pallas_call x1, Pallas kernels, local(): pl.pallas_call(functools.partial(backward_kernel, members // BACK), out_s...  5.18 us

profile of v2, /device:TPU:0, one launch (start us, length us, event | category | flops | bytes accessed | tf_op | source)
XLA Modules:
  0.0 33.3 jit_solution(13943387989875756950)
XLA Ops:
  0.0 28.1 %forward.1 = (f32[80,768]{1,0:T(8,128)}, bf16[20,80,720]{2,1,0:T(8,128)(2,1)}, bf16[48,80]{1,0:T(8,128)(2,1)}, bf16[512,256]{1,0:T(8,128)(2,1)}) custom-call(bf16[20,1,45,720]{3,2,1,0:T(8,128)(2,1)} %control.3, bf16[20,1,45,720]{3,2,1,0:T(8,128)(2,1)} %perturb.1, bf16[17]{0:T(256)(128)(2,1)} %lon_taps.1, bf16[17]{0:T(256)(128)(2,1)} %lat_taps.1, ...), custom_call_target="tpu_custom_call" | custom-call | tf_op jit(solution)/shard_map/forward/pallas_call | solution.py:569
  28.1 5.2 %backward.1 = f32[20,45,1,720]{3,2,1,0:T(1,128)} custom-call(bf16[20,1,45,720]{3,2,1,0:T(8,128)(2,1)} %control.3, f32[80,768]{1,0:T(8,128)} %get-tuple-element.9.spread_in, bf16[20,80,720]{2,1,0:T(8,128)(2,1)} %get-tuple-element.10.perturb_wide, bf16[48,80]{1,0:T(8,128)(2,1)} %get-tuple-element.11.lon_band_in, bf16[512,256]{1,0:T(8,128)(2,1)} %get-tuple-element.12.lat_band_in), custom_call_target="tpu_custom_call" | custom-call | tf_op jit(solution)/shard_map/backward/pallas_call | solution.py:585

commit v3 on v2

--- a/solution.py
+++ b/solution.py
@@ -469,7 +469,7 @@
         )
 
     def store(m):
-        return pltpu.make_async_copy(out.at[m], gradient.at[m], out_sem.at[m])
+        return pltpu.make_async_copy(out.at[m, 0:lon_cells], gradient.at[m], out_sem.at[m])
 
     pairs = ((spread_in, spread), (lon_band_in, lon_band), (lat_band_in, lat_band))
     firsts = [pltpu.make_async_copy(src, dst, first_sem.at[n]) for n, (src, dst) in enumerate(pairs)]
@@ -505,7 +505,7 @@
                 count = lanes.stop - lanes.start
                 first = (n * BACK + k) * rows
                 value = control_own[m, :, lanes].astype(F32) + smooth[first : first + lon_cells, 0:count]
-                out[m, :, :, lanes] = value[:, None, :]
+                out[m, 0:lon_cells, :, lanes] = value[:, None, :]
             store(m).start()
         return carry
 
@@ -593,7 +593,7 @@
             pltpu.VMEM((depth, width), F32),
             *bands,
             pltpu.VMEM((BACK * rows, width + PART), BF16),
-            pltpu.VMEM((members, lon_cells, 1, lat), F32),
+            pltpu.VMEM((members, rows, 1, lat), F32),
             dma((3,)),
             dma((2, members // BACK)),
             dma((members,)),

time: 33.5 us -> 33.5 us (level)
  no operation moved by 1% of the time
where the time goes in v3:
time: 33.5 us; the launch traced here: 33.3 us
  Pallas kernels  33.3 us (99%)
    pallas_call x1, Pallas kernels, local(): pl.pallas_call(functools.partial(forward_kernel, tiles, mems, groups), ou...  28.1 us
    pallas_call x1, Pallas kernels, local(): pl.pallas_call(functools.partial(backward_kernel, members // BACK), out_s...  5.18 us

profile of v3, /device:TPU:0, one launch (start us, length us, event | category | flops | bytes accessed | tf_op | source)
XLA Modules:
  0.0 33.3 jit_solution(7144684448469821757)
XLA Ops:
  0.0 28.1 %forward.1 = (f32[80,768]{1,0:T(8,128)}, bf16[20,80,720]{2,1,0:T(8,128)(2,1)}, bf16[48,80]{1,0:T(8,128)(2,1)}, bf16[512,256]{1,0:T(8,128)(2,1)}) custom-call(bf16[20,1,45,720]{3,2,1,0:T(8,128)(2,1)} %control.3, bf16[20,1,45,720]{3,2,1,0:T(8,128)(2,1)} %perturb.1, bf16[17]{0:T(256)(128)(2,1)} %lon_taps.1, bf16[17]{0:T(256)(128)(2,1)} %lat_taps.1, ...), custom_call_target="tpu_custom_call" | custom-call | tf_op jit(solution)/shard_map/forward/pallas_call | solution.py:569
  28.1 5.2 %backward.1 = f32[20,45,1,720]{3,2,1,0:T(1,128)} custom-call(bf16[20,1,45,720]{3,2,1,0:T(8,128)(2,1)} %control.3, f32[80,768]{1,0:T(8,128)} %get-tuple-element.9.spread_in, bf16[20,80,720]{2,1,0:T(8,128)(2,1)} %get-tuple-element.10.perturb_wide, bf16[48,80]{1,0:T(8,128)(2,1)} %get-tuple-element.11.lon_band_in, bf16[512,256]{1,0:T(8,128)(2,1)} %get-tuple-element.12.lat_band_in), custom_call_target="tpu_custom_call" | custom-call | tf_op jit(solution)/shard_map/backward/pallas_call | solution.py:585
